TPU v7x, 32 devices: a whole 2x2x4 slice. The times are simulated.
32 devices in a mesh: expert: 4 (over y, x), req: 8 (over z, core).
Axes of the slice: x: 2, y: 2, z: 4, core: 2. Of those that a mesh axis runs over, the one named last changes fastest.
Arguments:
- queries: bfloat16 [8192, 1024], P(('expert', 'req')), may hold values from -82 to 82
- self_kv: bfloat16 [8192, 2048], P(('expert', 'req')), may hold values from -4 to 4
- kv_pages: bfloat16 [32, 128, 2048], P(('expert', 'req')), may hold values from -4 to 4
- page_table: int32 [4, 8], P('expert'), may hold values from 0 to 7, as said below
- lengths: int32 [8192], P(('expert', 'req')), may hold values from 1 to 1024
- routes: int32 [8192, 2], P(('expert', 'req')), may hold values from 0 to 3, all different within a row
- residual: bfloat16 [8192, 1024], P(('expert', 'req')), may hold values from -20 to 20
- w_attn_out: bfloat16 [1024, 1024], replicated, may hold values from -0.1875 to 0.1875
- gain_attn: bfloat16 [1024], replicated, may hold values from 0.25 to 1.75
- w_router: bfloat16 [1024, 4], replicated, may hold values from -0.1875 to 0.1875
- w_in: bfloat16 [4, 1024, 2816], P('expert'), may hold values from -0.1875 to 0.1875
- w_out: bfloat16 [4, 1408, 1024], P('expert'), may hold values from -0.15625 to 0.15625
- gain_out: bfloat16 [1024], replicated, may hold values from 0.25 to 1.75
Outputs:
- layer_out: bfloat16 [8192, 1024], P(('expert', 'req'))
Inputs may be any that keep to these rules, and one draw needn't show every extreme that they name: Each row of page_table is a permutation of 0 to 7.
All inputs are finite; a program needn't handle non-finite values.
Results may differ from a plain program's by a relative error of at most 0.01.
Values may be sent and summed in bfloat16 or wider, within the bound.
A program may use at most 128 MiB of HBM per device.

v0:
```python
import math
import jax
import jax.numpy as jnp
from jax import lax
from jax.sharding import PartitionSpec as P

HEADS = 16
HEAD_DIM = 64
TOP = 2
PAGE = 128
HD = 1024
norm_eps = 1e-06


def block_size(total_count, largest):
    chosen = min(total_count, largest)
    while total_count % chosen:
        chosen -= 1
    return chosen


def key_positions(table_row, key_count, page_len):
    logical = jnp.arange(table_row.shape[0], dtype=jnp.int32)
    inverse = jnp.sum(
        jnp.where(table_row[:, None] == logical[None, :], logical[:, None], 0), axis=0
    )
    flat_index = jnp.arange(key_count, dtype=jnp.int32)
    page_index = flat_index // page_len
    logical_page = jnp.sum(
        jnp.where(page_index[:, None] == logical[None, :], inverse[None, :], 0), axis=1
    )
    return logical_page * page_len + flat_index % page_len


def rms_scale(values, gain_row):
    mean_square = jnp.mean(values * values, axis=-1, keepdims=True)
    return values * lax.rsqrt(mean_square + norm_eps) * gain_row.astype(jnp.float32)


def route_block(route_rows, cap_size, expert_count):
    onehot = (
        route_rows[:, :, None] == jnp.arange(expert_count, dtype=jnp.int32)[None, None, :]
    ).astype(jnp.int32)
    ordered = onehot.transpose(1, 0, 2).reshape(-1, expert_count)
    total = ordered.shape[0]
    before = jnp.arange(total)[:, None] > jnp.arange(total)[None, :]
    earlier = jnp.dot(
        before.astype(jnp.bfloat16),
        ordered.astype(jnp.bfloat16),
        preferred_element_type=jnp.float32,
    ).astype(jnp.int32)
    position = jnp.sum(earlier * ordered, axis=1).reshape(route_rows.shape[1], route_rows.shape[0])
    kept_mask = position < cap_size
    slot_ids = jnp.where(kept_mask, route_rows.T * cap_size + position, -1)
    return (onehot, kept_mask, slot_ids)


def on_device(
    queries,
    self_kv,
    kv_pages,
    page_table,
    lengths,
    routes,
    residual,
    w_attn_out,
    gain_attn,
    w_router,
    w_in,
    w_out,
    gain_out,
):
    row_count = queries.shape[0]
    scale_qk = 1.0 / math.sqrt(HEAD_DIM)
    table_row = page_table[0]
    page_rows = kv_pages.reshape(-1, kv_pages.shape[-1])
    query_h = queries.reshape(row_count, HEADS, HEAD_DIM)
    own_key = self_kv[:, :HD].reshape(row_count, HEADS, HEAD_DIM)
    own_value = self_kv[:, HD:].reshape(row_count, HEADS, HEAD_DIM)
    own_score = (
        jnp.einsum("rhd,rhd->hr", query_h, own_key, preferred_element_type=jnp.float32) * scale_qk
    )
    start_value = jnp.swapaxes(own_value, 0, 1).astype(jnp.float32)
    initial = (own_score, jnp.ones_like(own_score), start_value)
    page_piece = lax.all_gather(page_rows, "req", axis=0, tiled=True)
    piece_len = page_piece.shape[0]
    step_len = block_size(piece_len, 512)
    positions = key_positions(table_row, piece_len, PAGE)
    blocks = page_piece.reshape(piece_len // step_len, step_len, page_piece.shape[1])
    block_pos = positions.reshape(piece_len // step_len, step_len)

    def add_block(running, block_items):
        highest, weight_sum, weighted = running
        block_rows, block_place = block_items
        key_rows = block_rows[:, :HD].reshape(step_len, HEADS, HEAD_DIM)
        value_rows = block_rows[:, HD:].reshape(step_len, HEADS, HEAD_DIM)
        scores = (
            jnp.einsum("rhd,khd->hrk", query_h, key_rows, preferred_element_type=jnp.float32)
            * scale_qk
        )
        visible = block_place[None, :] < lengths[:, None]
        masked = jnp.where(visible[None], scores, -jnp.inf)
        new_high = jnp.maximum(highest, jnp.max(masked, axis=2))
        factor = jnp.exp(highest - new_high)
        weights = jnp.exp(masked - new_high[:, :, None])
        weight_sum = weight_sum * factor + jnp.sum(weights, axis=2)
        weighted = weighted * factor[:, :, None] + jnp.einsum(
            "hrk,khd->hrd",
            weights.astype(jnp.bfloat16),
            value_rows,
            preferred_element_type=jnp.float32,
        )
        return ((new_high, weight_sum, weighted), None)

    result, unused = lax.scan(add_block, initial, (blocks, block_pos))
    highest, weight_sum, weighted = result
    attended = (
        (weighted / weight_sum[:, :, None])
        .transpose(1, 0, 2)
        .reshape(row_count, HD)
        .astype(jnp.bfloat16)
    )
    residual_sum = residual.astype(jnp.float32) + jnp.dot(
        attended, w_attn_out, preferred_element_type=jnp.float32
    )
    normed = rms_scale(residual_sum, gain_attn).astype(jnp.bfloat16)
    logits = jnp.dot(normed, w_router, preferred_element_type=jnp.float32)
    experts_all = w_router.shape[1]
    cap_size = (5 * row_count * TOP + 4 * experts_all - 1) // (4 * experts_all)
    onehot, kept_mask, slot_ids = route_block(routes, cap_size, experts_all)
    picked = jnp.sum(jnp.where(onehot > 0, logits[:, None, :], 0.0), axis=2)
    gate_values = jax.nn.sigmoid(picked - picked[:, ::-1])
    slot_range = jnp.arange(experts_all * cap_size, dtype=jnp.int32)
    assign = jnp.sum(
        (slot_ids[:, None, :] == slot_range[None, :, None]).astype(jnp.bfloat16), axis=0
    )
    model_width = normed.shape[1]
    buffer = (
        jnp.dot(assign, normed, preferred_element_type=jnp.float32)
        .astype(jnp.bfloat16)
        .reshape(experts_all, cap_size, model_width)
    )
    arrived = lax.all_to_all(buffer, "expert", split_axis=0, concat_axis=0, tiled=True)
    slot_count = arrived.shape[1]
    local_experts = w_in.shape[0]
    hidden_width = w_out.shape[1]
    grouped = arrived.reshape(-1, local_experts, slot_count, model_width)
    inner_act = jnp.einsum("slnd,ldf->slnf", grouped, w_in, preferred_element_type=jnp.float32)
    hidden = (
        jax.nn.gelu(inner_act[..., :hidden_width], approximate=True) * inner_act[..., hidden_width:]
    ).astype(jnp.bfloat16)
    outcome = jnp.einsum(
        "slnf,lfd->slnd", hidden, w_out, preferred_element_type=jnp.float32
    ).astype(jnp.bfloat16)
    expert_done = outcome.reshape(-1, slot_count, model_width)
    collected = lax.all_to_all(expert_done, "expert", split_axis=0, concat_axis=0, tiled=True)
    flat_rows = collected.reshape(-1, model_width)
    picked_rows = flat_rows[jnp.maximum(slot_ids, 0)]
    gate_kept = jnp.where(kept_mask, gate_values.T, 0.0)
    mixture = jnp.sum(picked_rows.astype(jnp.float32) * gate_kept[:, :, None], axis=0)
    return rms_scale(residual_sum + mixture, gain_out).astype(jnp.bfloat16)


def solution(mesh):
    in_specs = (
        P(("expert", "req"), None),
        P(("expert", "req"), None),
        P(("expert", "req"), None, None),
        P("expert", None),
        P(("expert", "req")),
        P(("expert", "req"), None),
        P(("expert", "req"), None),
        P(),
        P(),
        P(),
        P("expert", None, None),
        P("expert", None, None),
        P(),
    )
    out_specs = P(("expert", "req"), None)
    return jax.shard_map(
        on_device, mesh=mesh, in_specs=in_specs, out_specs=out_specs, check_vma=False
    )
```

profile of v0, /device:TPU:0, one launch (start us, length us, event | category | flops | bytes accessed | tf_op | source)
XLA Modules:
  0.0 183.1 jit_solution(15243660066245395391)
XLA Ops:
  6.5 0.0 copy-start
  6.5 0.0 all-gather.3.cloned.1.call-start
  6.6 0.7 all-gather.3.cloned.1.call-update
  7.3 2.5 %slice_convert_fusion = (f32[256,1024]{1,0:T(8,128)}, bf16[256,1024]{1,0:T(8,128)(2,1)S(1)}) fusion(bf16[256,2048]{1,0:T(8,128)(2,1)} %param.16), kind=kLoop, calls=%fused_computation.55 | loop fusion | flops 262144 | bytes 2621440 | tf_op jit(solution)/shard_map/convert_element_type | solution.py:83
  9.7 1.0 copy.42
  10.7 1.2 copy.40
  12.0 2.6 %copy.29 = f32[256,1024]{0,1:T(8,128)} copy(f32[256,1024]{1,0:T(8,128)} %get-tuple-element.119) | data formatting | bytes 2097152 | tf_op jit(solution)/shard_map/convert_element_type | solution.py:83
  14.6 0.0 copy-done.14
  14.6 0.1 select_reduce_fusion.2
  14.7 0.1 select_reduce_fusion
  14.8 0.0 copy-done.12
  14.8 0.6 convert_element_type.81
  15.4 0.3 fusion.41
  15.7 0.6 maximum_bitcast_fusion
  16.3 1.0 fusion.43
  17.3 1.2 fusion.42
  18.5 0.6 fusion.44
  19.1 0.6 broadcast_multiply_fusion
  19.7 39.1 %all-gather.3.cloned.1.call-done = bf16[1,1024,2048]{2,1,0:T(8,128)(2,1)} async-done(((bf16[1,128,2048]{2,1,0:T(8,128)(2,1)}), bf16[1,1024,2048]{2,1,0:T(8,128)(2,1)}) %all-gather.3.cloned.1.call-update) | async-done | bytes 4194320 | tf_op jit(solution)/shard_map/all_gather | solution.py:85
  58.9 0.0 copy-done.8
  58.9 54.3 %while.15 = (s32[]{:T(128)}, f32[16,256]{1,0:T(8,128)}, f32[16,256]{1,0:T(8,128)}, f32[16,256,64]{1,2,0:T(8,128)}, s32[2,512]{1,0:T(2,128)}, /*index=5*/s32[256]...) while((s32[]{:T(128)}, f32[16,256]{1,0:T(8,128)}, ...), condition=%wide.region_5.6_spmd.clone, body=%wide.region_2.5_spmd.clone.sunk | while | flops 560607232 | bytes 76881064 | solution.py:115
  58.9 0.7 constant_dynamic-slice_fusion.4
  59.5 0.8 broadcast_compare_fusion.3
  60.4 3.1 %constant_dynamic-slice_fusion.5 = bf16[1,512,2048]{2,1,0:T(8,128)(2,1)} fusion(bf16[2,512,2048]{2,1,0:T(8,128)(2,1)} %get-tuple-element.210, s32[]{:T(128)} %get-tuple-element.194), kind=kLoop, calls=%fused_computation.13.clone.1 | loop fusion | bytes 4194308 | tf_op jit(solution)/shard_map/while/body/jit(dynamic_index_in_dim)/dynamic_slice | solution.py:115
  63.5 3.9 %copy.46 = bf16[1,512,2048]{1,2,0:T(8,128)(2,1)} copy(bf16[1,512,2048]{2,1,0:T(8,128)(2,1)} %constant_dynamic-slice_fusion.5) | data formatting | bytes 4194304 | tf_op jit(solution)/shard_map/while/body/jit(dynamic_index_in_dim)/dynamic_slice | solution.py:115
  67.4 2.6 %fusion.80 = (bf16[512,1024]{0,1:T(8,128)(2,1)}, bf16[512,1024]{0,1:T(8,128)(2,1)S(1)}) fusion(bf16[512,2048]{0,1:T(8,128)(2,1)} %bitcast.102), kind=kLoop, calls=%fused_computation.94.clone.1 | loop fusion | bytes 4194304 | tf_op jit(solution)/shard_map/while/body/eval_jaxpr/slice | solution.py:96
  70.1 1.5 fusion.81
  71.6 3.2 %copy-done.1 = f32[16,512,256]{2,1,0:T(8,128)} copy-done((f32[16,512,256]{2,1,0:T(8,128)}, f32[16,512,256]{2,1,0:T(8,128)S(1)}, u32[]{:S(2)}) %copy-start.1) | copy-done | bytes 8388632 | tf_op jit(solution)/shard_map/while
  74.8 2.3 %fusion.82 = f32[16,256]{1,0:T(8,128)} fusion(f32[16,512,256]{2,1,0:T(8,128)S(1)} %get-tuple-element.180, f32[16,256]{1,0:T(8,128)S(1)} %max.10, pred[256,512]{0,1:T(8,128)(4,1)S(1)} %broadcast_compare_fusion.3), kind=kLoop, calls=%fused_computation.4.clone.1 | loop fusion | flops 8384512 | bytes 8552448 | tf_op jit(solution)/shard_map/while/body/eval_jaxpr/reduce_sum | solution.py:106
  77.1 1.3 fusion.83
  78.4 7.0 %fusion.84 = f32[16,256,64]{1,2,0:T(8,128)} fusion(bf16[512,16,64]{0,2,1:T(8,128)(2,1)} %bitcast.105, f32[16,512,256]{2,1,0:T(8,128)} %copy-done.1, f32[16,256]{1,0:T(8,128)S(1)} %max.10, pred[256,512]{0,1:T(8,128)(4,1)S(1)} %broadcast_compare_fusion.3, f32[16,256,64]{1,2,0:T(8,128)} %get-tuple-element.197, f32[16,256]{1,0:T(8,128)S(1)} %get-tuple-element.183), kind=kOutput, calls=%fused_computation.8.clone.1 | convolution fusion | flops 277348352 | bytes 11698176 | tf_op jit(solution)/shard_map/while/body/eval_jaxpr/hrk,khd->hrd/dot_general | solution.py:107
  85.4 0.6 copy.56
  86.0 0.7 constant_dynamic-slice_fusion.4
  86.7 0.8 broadcast_compare_fusion.3
  87.5 3.1 %constant_dynamic-slice_fusion.5 = bf16[1,512,2048]{2,1,0:T(8,128)(2,1)} fusion(bf16[2,512,2048]{2,1,0:T(8,128)(2,1)} %get-tuple-element.210, s32[]{:T(128)} %get-tuple-element.194), kind=kLoop, calls=%fused_computation.13.clone.1 | loop fusion | bytes 4194308 | tf_op jit(solution)/shard_map/while/body/jit(dynamic_index_in_dim)/dynamic_slice | solution.py:115
  90.7 3.9 %copy.46 = bf16[1,512,2048]{1,2,0:T(8,128)(2,1)} copy(bf16[1,512,2048]{2,1,0:T(8,128)(2,1)} %constant_dynamic-slice_fusion.5) | data formatting | bytes 4194304 | tf_op jit(solution)/shard_map/while/body/jit(dynamic_index_in_dim)/dynamic_slice | solution.py:115
  94.6 2.6 %fusion.80 = (bf16[512,1024]{0,1:T(8,128)(2,1)}, bf16[512,1024]{0,1:T(8,128)(2,1)S(1)}) fusion(bf16[512,2048]{0,1:T(8,128)(2,1)} %bitcast.102), kind=kLoop, calls=%fused_computation.94.clone.1 | loop fusion | bytes 4194304 | tf_op jit(solution)/shard_map/while/body/eval_jaxpr/slice | solution.py:96
  97.2 1.5 fusion.81
  98.7 0.0 copy-start.1
  98.7 0.0 copy-done.3
  98.8 3.2 %copy-done.1 = f32[16,512,256]{2,1,0:T(8,128)} copy-done((f32[16,512,256]{2,1,0:T(8,128)}, f32[16,512,256]{2,1,0:T(8,128)S(1)}, u32[]{:S(2)}) %copy-start.1) | copy-done | bytes 8388632 | tf_op jit(solution)/shard_map/while
  102.0 2.3 %fusion.82 = f32[16,256]{1,0:T(8,128)} fusion(f32[16,512,256]{2,1,0:T(8,128)S(1)} %get-tuple-element.180, f32[16,256]{1,0:T(8,128)S(1)} %max.10, pred[256,512]{0,1:T(8,128)(4,1)S(1)} %broadcast_compare_fusion.3), kind=kLoop, calls=%fused_computation.4.clone.1 | loop fusion | flops 8384512 | bytes 8552448 | tf_op jit(solution)/shard_map/while/body/eval_jaxpr/reduce_sum | solution.py:106
  104.2 1.4 fusion.83
  105.6 7.0 %fusion.84 = f32[16,256,64]{1,2,0:T(8,128)} fusion(bf16[512,16,64]{0,2,1:T(8,128)(2,1)} %bitcast.105, f32[16,512,256]{2,1,0:T(8,128)} %copy-done.1, f32[16,256]{1,0:T(8,128)S(1)} %max.10, pred[256,512]{0,1:T(8,128)(4,1)S(1)} %broadcast_compare_fusion.3, f32[16,256,64]{1,2,0:T(8,128)} %get-tuple-element.197, f32[16,256]{1,0:T(8,128)S(1)} %get-tuple-element.183), kind=kOutput, calls=%fused_computation.8.clone.1 | convolution fusion | flops 277348352 | bytes 11698176 | tf_op jit(solution)/shard_map/while/body/eval_jaxpr/hrk,khd->hrd/dot_general | solution.py:107
  112.6 0.6 copy.56
  113.2 1.5 divide_convert_fusion
  114.7 0.0 slice-start.1
  114.7 2.7 %multiply_reduce_fusion.1 = (f32[256]{0:T(256)S(1)}, f32[256,1024]{1,0:T(8,128)S(1)}) fusion(bf16[256,1024]{0,1:T(8,128)(2,1)S(1)} %bitcast.110, bf16[1024,1024]{1,0:T(8,128)(2,1)} %param.22, bf16[256,1024]{1,0:T(8,128)(2,1)} %param.21), kind=kOutput, calls=%fused_computation.51 | convolution fusion | flops 537919232 | bytes 4195328 | tf_op jit(solution)/shard_map/dot_general | solution.py:123
  117.4 1.0 copy-done.2
  118.4 0.6 convolution_convert_fusion
  119.0 20.6 %all_to_all.10 = bf16[4,160,1024]{2,1,0:T(8,128)(2,1)S(1)} all-to-all(bf16[4,160,1024]{2,1,0:T(8,128)(2,1)S(1)} %bitcast.107), channel_id=1, replica_groups=mesh['expert'=4,'req'=8] {'expert'}, dimensions={0} | all-to-all | bytes 2621440 | tf_op jit(solution)/shard_map/all_to_all | solution.py:143
  139.6 0.0 slice-done
  139.6 3.9 %fusion.14 = f32[4,1,160,2816]{3,2,0,1:T(8,128)S(1)} fusion(bf16[4,160,1024]{2,1,0:T(8,128)(2,1)S(1)} %all_to_all.10, bf16[1,1024,2816]{2,1,0:T(8,128)(2,1)S(1)} %bitcast.116), kind=kOutput, calls=%fused_computation.20 | convolution fusion | flops 3690987520 | bytes 14286848 | tf_op jit(solution)/shard_map/slnd,ldf->slnf/dot_general | solution.py:148
  143.5 0.0 copy-start.13
  143.5 0.0 copy-start.10
  143.5 3.6 %fusion.34 = bf16[4,160,1024]{2,1,0:T(8,128)(2,1)} fusion(bf16[1,1408,1024]{2,1,0:T(8,128)(2,1)S(1)} %copy-done, f32[4,1,160,2816]{3,2,0,1:T(8,128)S(1)} %fusion.14), kind=kOutput, calls=%fused_computation.39 | convolution fusion | flops 1855160320 | bytes 11403264 | tf_op jit(solution)/shard_map/slnf,lfd->slnd/dot_general | solution.py:152
  147.2 4.4 %all-to-all-start.1 = ((bf16[4,160,1024]{2,1,0:T(8,128)(2,1)}), bf16[4,160,1024]{2,1,0:T(8,128)(2,1)}, u32[]{:S(2)}, u32[]{:S(2)}) async-start(bf16[4,160,1024]{2,1,0:T(8,128)(2,1)} %fusion.34), calls=%async_computation.1 | async-start | bytes 2621440 | tf_op jit(solution)/shard_map/all_to_all | solution.py:156
  151.7 1.5 fusion.56
  153.2 0.1 rev.3
  153.4 13.9 %all-to-all-done.1 = bf16[4,160,1024]{2,1,0:T(8,128)(2,1)} async-done(((bf16[4,160,1024]{2,1,0:T(8,128)(2,1)}), bf16[4,160,1024]{2,1,0:T(8,128)(2,1)}, u32[]{:S(2)}, u32[]{:S(2)}) %all-to-all-start.1) | async-done | bytes 1310752 | tf_op jit(solution)/shard_map/all_to_all | solution.py:156
  167.3 5.0 %gather_fusion = bf16[512,1024]{1,0:T(8,128)(2,1)} fusion(bf16[640,1024]{1,0:T(8,128)(2,1)} %bitcast.25, s32[1024]{0:T(1024)S(1)} %pad_clamp_fusion), kind=kCustom, calls=%fused_computation | custom fusion | bytes 2099200 | tf_op jit(solution)/shard_map/gather | solution.py:158
  172.3 1.6 fusion.28
  173.8 1.4 multiply_reduce_fusion
  175.3 1.0 multiply_convert_fusion
  (41 shorter events, 0.2 us)
Async XLA Ops:
  6.5 137.0 %copy-start = (bf16[1,1408,1024]{2,1,0:T(8,128)(2,1)S(1)}, bf16[1,1408,1024]{2,1,0:T(8,128)(2,1)}, u32[]{:S(2)}) copy-start(bf16[1,1408,1024]{2,1,0:T(8,128)(2,1)} %param.26) | copy-start | bytes 8650756
  6.5 8.1 %copy-start.14 = (s32[1,8]{1,0:T(1,128)S(1)}, s32[1,8]{1,0:T(1,128)}, u32[]{:S(2)}) copy-start(s32[1,8]{1,0:T(1,128)} %param.18) | copy-start | bytes 100
  6.5 8.3 %copy-start.12 = (bf16[1024]{0:T(1024)(128)(2,1)S(1)}, bf16[1024]{0:T(1024)(128)(2,1)}, u32[]{:S(2)}) copy-start(bf16[1024]{0:T(1024)(128)(2,1)} %param.23) | copy-start | bytes 6148
  6.5 8.8 %copy-start.6 = (s32[256,2]{0,1:T(2,128)S(1)}, s32[256,2]{0,1:T(2,128)}, u32[]{:S(2)}) copy-start(s32[256,2]{0,1:T(2,128)} %param.20) | copy-start | bytes 6148
  6.5 52.3 %all-gather.3.cloned.1.call-start = ((), (), s32[]{:S(2)}) async-start(), calls=%async_computation.2 | async-start | bytes 4718592 | tf_op jit(solution)/shard_map/all_gather | solution.py:85
  15.7 43.2 %copy-start.8 = (s32[2,256]{1,0:T(2,128)}, s32[2,256]{1,0:T(2,128)S(1)}, u32[]{:S(2)}) copy-start(s32[2,256]{1,0:T(2,128)S(1)} %reshape.127) | copy-start | bytes 6148
  70.1 1.5 copy-start.3
  71.6 3.2 %copy-start.1 = (f32[16,512,256]{2,1,0:T(8,128)}, f32[16,512,256]{2,1,0:T(8,128)S(1)}, u32[]{:S(2)}) copy-start(f32[16,512,256]{2,1,0:T(8,128)S(1)} %get-tuple-element.180) | copy-start | bytes 25165828 | tf_op jit(solution)/shard_map/while
  97.2 1.5 copy-start.3
  98.7 3.2 %copy-start.1 = (f32[16,512,256]{2,1,0:T(8,128)}, f32[16,512,256]{2,1,0:T(8,128)S(1)}, u32[]{:S(2)}) copy-start(f32[16,512,256]{2,1,0:T(8,128)S(1)} %get-tuple-element.180) | copy-start | bytes 25165828 | tf_op jit(solution)/shard_map/while
  113.2 5.2 %copy-start.4 = (bf16[640,256]{1,0:T(8,128)(2,1)S(1)}, bf16[640,256]{1,0:T(8,128)(2,1)}, u32[]{:S(2)}) copy-start(bf16[640,256]{1,0:T(8,128)(2,1)} %fusion.43) | copy-start | bytes 983044
  113.2 5.2 %copy-start.5 = (f32[1024]{0:T(1024)S(1)}, f32[1024]{0:T(1024)}, u32[]{:S(2)}) copy-start(f32[1024]{0:T(1024)} %convert_element_type.81) | copy-start | bytes 12292
  113.2 26.4 %slice-start = ((s8[5767168]{0:T(1024)(128)(4,1)}), s8[4194304]{0:T(1024)(128)(4,1)S(1)}, s32[]{:S(2)}) async-start(s8[5767168]{0:T(1024)(128)(4,1)} %bitcast.115), calls=%async_computation.3 | async-start | bytes 8388608
  114.7 24.9 %slice-start.1 = ((s8[5767168]{0:T(1024)(128)(4,1)}), s8[1572864]{0:T(1024)(128)(4,1)S(1)}, s32[]{:S(2)}) async-start(s8[5767168]{0:T(1024)(128)(4,1)} %bitcast.115), calls=%async_computation.4 | async-start | bytes 3145728
  117.4 1.0 copy-start.2
  143.5 8.1 %copy-start.11 = (s32[1,2,2,128]{3,2,1,0:T(2,128)S(1)}, s32[1,2,2,128]{3,2,1,0:T(2,128)}, u32[]{:S(2)}) copy-start(s32[1,2,2,128]{3,2,1,0:T(2,128)} %get-tuple-element.113) | copy-start | bytes 6148
  143.5 8.1 %copy-start.13 = (bf16[1024]{0:T(1024)(128)(2,1)S(1)}, bf16[1024]{0:T(1024)(128)(2,1)}, u32[]{:S(2)}) copy-start(bf16[1024]{0:T(1024)(128)(2,1)} %param.27) | copy-start | bytes 6148
  143.5 8.1 %copy-start.10 = (bf16[1024,4]{0,1:T(4,128)(2,1)S(1)}, bf16[1024,4]{0,1:T(4,128)(2,1)}, u32[]{:S(2)}) copy-start(bf16[1024,4]{0,1:T(4,128)(2,1)} %param.24) | copy-start | bytes 24580
  147.2 6.0 %copy-start.7 = (s32[256,2]{0,1:T(2,128)S(1)}, s32[256,2]{0,1:T(2,128)}, u32[]{:S(2)}) copy-start(s32[256,2]{0,1:T(2,128)} %param.20) | copy-start | bytes 6148
  147.2 6.1 %copy-start.9 = (s32[2,256]{1,0:T(2,128)S(1)}, s32[2,256]{1,0:T(2,128)}, u32[]{:S(2)}) copy-start(s32[2,256]{1,0:T(2,128)} %copy-done.8) | copy-start | bytes 6148
  147.2 20.1 %all-to-all-start.1 = ((bf16[4,160,1024]{2,1,0:T(8,128)(2,1)}), bf16[4,160,1024]{2,1,0:T(8,128)(2,1)}, u32[]{:S(2)}, u32[]{:S(2)}) async-start(bf16[4,160,1024]{2,1,0:T(8,128)(2,1)} %fusion.34), calls=%async_computation.1 | async-start | bytes 2621440 | tf_op jit(solution)/shard_map/all_to_all | solution.py:156
Sparse Core Ops, SparseCore 0:
  9.0 49.8 all-gather.2
where the time goes:
time: 184 us; the launch traced here: 183 us
  waiting for transfers between devices  53.7 us (29%)
  local copies, waits for them, and re-layouts  39.4 us (21%)
  matrix products  29.6 us (16%)
  other arithmetic  21.7 us (12%)
  blocking collectives  20.6 us (11%)
  between operations  13.6 us (7%)
  starting transfers between devices  4.44 us (2%)
    all_gather x1, waiting for transfers between devices, on_device(): page_piece = lax.all_gather(page_rows, 'req', axis=0, tiled=True)  39.1 us
    all_to_all x1, blocking collectives, on_device(): lax.all_to_all(buffer, 'expert', split_axis=0, concat_axis=0, tiled=True)  20.6 us
    dynamic_slice x6, local copies, waits for them, and re-layouts, on_device(): result, unused = lax.scan(add_block, initial, (blocks, block_pos))  15.5 us
    dot_general x2, matrix products, add_block(): jnp.einsum('hrk,khd->hrd', weights.astype(jnp.bfloat16), value_rows, pref...  14 us
    all_to_all x1, waiting for transfers between devices, on_device(): lax.all_to_all(expert_done, 'expert', split_axis=0, concat_axis=0, tiled=...  13.9 us
    while x10, local copies, waits for them, and re-layouts  7.6 us
    slice x2, local copies, waits for them, and re-layouts, add_block(): value_rows = block_rows[:, HD:].reshape(step_len, HEADS, HEAD_DIM)  5.29 us
    gather x1, local copies, waits for them, and re-layouts, on_device(): picked_rows = flat_rows[jnp.maximum(slot_ids, 0)]  4.97 us
  transfers between devices with their start and end apart: 2, of which 2 were waited for; matrix products, arithmetic and copies ran while one was open for 8% of the time, Pallas kernels for 0%

commit v1 on v0

--- a/solution.py
+++ b/solution.py
@@ -10,6 +10,24 @@
 PAGE = 128
 HD = 1024
 norm_eps = 1e-06
+
+
+def ring_gather(value, axis, dim):
+    ways, here, hop = (lax.axis_size(axis), lax.axis_index(axis), value.shape[dim])
+    shape = [n * ways if d == dim else n for d, n in enumerate(value.shape)]
+    full = lax.dynamic_update_slice_in_dim(
+        jnp.zeros(shape, value.dtype), value, here * hop, axis=dim
+    )
+    going_up = going_down = value
+    for far in range(1, ways // 2 + 1):
+        going_up = lax.ppermute(going_up, axis, [(d, (d + 1) % ways) for d in range(ways)])
+        full = lax.dynamic_update_slice_in_dim(full, going_up, (here - far) % ways * hop, axis=dim)
+        if 2 * far < ways:
+            going_down = lax.ppermute(going_down, axis, [(d, (d - 1) % ways) for d in range(ways)])
+            full = lax.dynamic_update_slice_in_dim(
+                full, going_down, (here + far) % ways * hop, axis=dim
+            )
+    return full
 
 
 def block_size(total_count, largest):
@@ -82,7 +100,7 @@
     )
     start_value = jnp.swapaxes(own_value, 0, 1).astype(jnp.float32)
     initial = (own_score, jnp.ones_like(own_score), start_value)
-    page_piece = lax.all_gather(page_rows, "req", axis=0, tiled=True)
+    page_piece = ring_gather(page_rows, "req", 0)
     piece_len = page_piece.shape[0]
     step_len = block_size(piece_len, 512)
     positions = key_positions(table_row, piece_len, PAGE)

time: 184 us -> 169 us (0.918)
  the two profiles are of different devices: /device:TPU:0 before, /device:TPU:8 now
where the time goes in v1:
time: 169 us; the launch traced here: 168 us
  local copies, waits for them, and re-layouts  52.7 us (31%)
  matrix products  29.5 us (17%)
  waiting for transfers between devices  27 us (16%)
  blocking collectives  21.8 us (13%)
  other arithmetic  21.5 us (13%)
  starting transfers between devices  15.3 us (9%)
    all_to_all x1, blocking collectives, on_device(): lax.all_to_all(buffer, 'expert', split_axis=0, concat_axis=0, tiled=True)  21.8 us
    all_to_all x1, waiting for transfers between devices, on_device(): lax.all_to_all(expert_done, 'expert', split_axis=0, concat_axis=0, tiled=...  15.5 us
    dynamic_slice x6, local copies, waits for them, and re-layouts, on_device(): result, unused = lax.scan(add_block, initial, (blocks, block_pos))  15.5 us
    dot_general x2, matrix products, add_block(): jnp.einsum('hrk,khd->hrd', weights.astype(jnp.bfloat16), value_rows, pref...  13.9 us
    ppermute x4, waiting for transfers between devices, ring_gather(): lax.ppermute(going_up, axis, [(d, (d + 1) % ways) for d in range(ways)])  10 us
    while x10, local copies, waits for them, and re-layouts  7.57 us
    ppermute x4, starting transfers between devices, ring_gather(): lax.ppermute(going_up, axis, [(d, (d + 1) % ways) for d in range(ways)])  7.48 us
    dynamic_update_slice x4, local copies, waits for them, and re-layouts, ring_gather(): lax.dynamic_update_slice_in_dim(full, going_up, (here - far) % ways * hop...  5.5 us
  transfers between devices with their start and end apart: 8, of which 5 were waited for; matrix products, arithmetic and copies ran while one was open for 16% of the time, Pallas kernels for 0%

profile of v1, /device:TPU:8, one launch (start us, length us, event | category | flops | bytes accessed | tf_op | source)
XLA Modules:
  0.0 168.1 jit_solution(6931001897559784297)
XLA Ops:
  0.1 1.7 %collective-permute-start.1 = (bf16[128,2048]{1,0:T(8,128)(2,1)}, bf16[128,2048]{1,0:T(8,128)(2,1)}, u32[]{:S(2)}, u32[]{:S(2)}) collective-permute-start(bf16[128,2048]{1,0:T(8,128)(2,1)} %bitcast.113), channel_id=1, source_target_pairs={{0,7},{1,0},{2,1},{3,2},{4,3},{5,4},{6,5},{7,6},{8,15},{9,8},{10,9... | collective-permute-start | bytes 1572872 | tf_op jit(solution)/shard_map/ppermute | solution.py:26
  1.8 2.3 %slice_convert_fusion = (f32[256,1024]{1,0:T(8,128)}, bf16[256,1024]{1,0:T(8,128)(2,1)S(1)}) fusion(bf16[256,2048]{1,0:T(8,128)(2,1)} %param.16), kind=kLoop, calls=%fused_computation.55 | loop fusion | flops 262144 | bytes 2621440 | tf_op jit(solution)/shard_map/convert_element_type | solution.py:101
  4.1 1.0 copy.42
  5.1 1.2 copy.40
  6.6 0.6 fusion.44
  7.2 1.2 fusion.42
  8.7 0.6 broadcast_multiply_fusion
  9.3 0.6 maximum_bitcast_fusion
  9.9 2.6 %collective-permute-done = bf16[128,2048]{1,0:T(8,128)(2,1)} collective-permute-done((bf16[128,2048]{1,0:T(8,128)(2,1)}, bf16[128,2048]{1,0:T(8,128)(2,1)}, u32[]{:S(2)}, u32[]{:S(2)}) %collective-permute-start) | collective-permute-done | bytes 524320 | tf_op jit(solution)/shard_map/ppermute | solution.py:23
  12.4 2.5 %broadcast_in_dim.93 = bf16[1024,2048]{1,0:T(8,128)(2,1)} broadcast(bf16[]{:T(256)} %constant.112.clone.1), dimensions={} | broadcast | bytes 4194306 | tf_op jit(solution)/shard_map/broadcast_in_dim | solution.py:19
  14.9 0.8 constant_dynamic-update-slice_fusion.7
  15.7 1.8 %collective-permute-start.3 = (bf16[128,2048]{1,0:T(8,128)(2,1)}, bf16[128,2048]{1,0:T(8,128)(2,1)}, u32[]{:S(2)}, u32[]{:S(2)}) collective-permute-start(bf16[128,2048]{1,0:T(8,128)(2,1)} %collective-permute-done.1), channel_id=1, source_target_pairs={{0,7},{1,0},{2,1},{3,2},{4,3},{5,4},{6,5},{7,6},{8,15},{9,8},{10,9... | collective-permute-start | bytes 1572872 | tf_op jit(solution)/shard_map/ppermute | solution.py:26
  17.5 1.0 fusion.43
  18.5 2.6 %copy.29 = f32[256,1024]{0,1:T(8,128)} copy(f32[256,1024]{1,0:T(8,128)} %get-tuple-element.119) | data formatting | bytes 2097152 | tf_op jit(solution)/shard_map/convert_element_type | solution.py:101
  21.1 0.6 convert_element_type.81
  21.7 4.7 %collective-permute-start.4 = (bf16[128,2048]{1,0:T(8,128)(2,1)}, bf16[128,2048]{1,0:T(8,128)(2,1)S(1)}, u32[]{:S(2)}, u32[]{:S(2)}) collective-permute-start(bf16[128,2048]{1,0:T(8,128)(2,1)} %collective-permute-done.2), channel_id=1, source_target_pairs={{0,1},{1,2},{2,3},{3,4},{4,5},{5,6},{6,7},{7,0},{8,9},{9,10},{10,1... | collective-permute-start | bytes 1572872 | tf_op jit(solution)/shard_map/ppermute | solution.py:23
  26.4 1.9 %constant_dynamic-update-slice_fusion.6 = bf16[1024,2048]{1,0:T(8,128)(2,1)} fusion(bf16[1024,2048]{1,0:T(8,128)(2,1)} %constant_dynamic-update-slice_fusion.7, bf16[128,2048]{1,0:T(8,128)(2,1)} %collective-permute-done, s32[]{:T(128)S(6)} %select_n.102), kind=kLoop, calls=%fused_computation.92 | loop fusion | bytes 1048580 | tf_op jit(solution)/shard_map/dynamic_update_slice | solution.py:24
  28.3 1.9 %constant_dynamic-update-slice_fusion.5 = bf16[1024,2048]{1,0:T(8,128)(2,1)} fusion(bf16[1024,2048]{1,0:T(8,128)(2,1)} %constant_dynamic-update-slice_fusion.6, bf16[128,2048]{1,0:T(8,128)(2,1)} %collective-permute-done.1, s32[]{:T(128)S(6)} %select_n.104), kind=kLoop, calls=%fused_computation.91 | loop fusion | bytes 1048580 | tf_op jit(solution)/shard_map/dynamic_update_slice | solution.py:27
  30.2 1.9 %constant_dynamic-update-slice_fusion.4 = bf16[1024,2048]{1,0:T(8,128)(2,1)} fusion(bf16[1024,2048]{1,0:T(8,128)(2,1)} %constant_dynamic-update-slice_fusion.5, bf16[128,2048]{1,0:T(8,128)(2,1)} %collective-permute-done.2, s32[]{:T(128)S(6)} %select_n.106), kind=kLoop, calls=%fused_computation.90 | loop fusion | bytes 1048580 | tf_op jit(solution)/shard_map/dynamic_update_slice | solution.py:24
  32.1 1.4 collective-permute-done.4
  33.6 2.7 %collective-permute-start.6 = (bf16[128,2048]{1,0:T(8,128)(2,1)S(1)}, bf16[128,2048]{1,0:T(8,128)(2,1)S(1)}, u32[]{:S(2)}, u32[]{:S(2)}) collective-permute-start(bf16[128,2048]{1,0:T(8,128)(2,1)S(1)} %collective-permute-done.4), channel_id=1, source_target_pairs={{0,1},{1,2},{2,3},{3,4},{4,5},{5,6},{6,7},{7,0},{8,9},{9,10},{10,1... | collective-permute-start | bytes 1572872 | tf_op jit(solution)/shard_map/ppermute | solution.py:23
  36.3 1.9 %constant_dynamic-update-slice_fusion.3 = bf16[1024,2048]{1,0:T(8,128)(2,1)} fusion(bf16[1024,2048]{1,0:T(8,128)(2,1)} %constant_dynamic-update-slice_fusion.4, bf16[128,2048]{1,0:T(8,128)(2,1)} %collective-permute-done.3, s32[]{:T(128)S(6)} %select_n.108), kind=kLoop, calls=%fused_computation.89 | loop fusion | bytes 1048580 | tf_op jit(solution)/shard_map/dynamic_update_slice | solution.py:27
  38.2 0.8 constant_dynamic-update-slice_fusion.2
  39.0 1.5 collective-permute-done.5
  40.5 0.8 constant_dynamic-update-slice_fusion.1
  41.3 6.0 %collective-permute-done.6 = bf16[128,2048]{1,0:T(8,128)(2,1)S(1)} collective-permute-done((bf16[128,2048]{1,0:T(8,128)(2,1)S(1)}, bf16[128,2048]{1,0:T(8,128)(2,1)S(1)}, u32[]{:S(2)}, u32[]{:S(2)}) %collective-permute-start.6) | collective-permute-done | bytes 524320 | tf_op jit(solution)/shard_map/ppermute | solution.py:23
  47.3 0.8 constant_dynamic-update-slice_fusion
  48.1 54.2 %while.15 = (s32[]{:T(128)}, f32[16,256]{1,0:T(8,128)}, f32[16,256]{1,0:T(8,128)}, f32[16,256,64]{1,2,0:T(8,128)}, s32[2,512]{1,0:T(2,128)}, /*index=5*/s32[256]...) while((s32[]{:T(128)}, f32[16,256]{1,0:T(8,128)}, ...), condition=%wide.region_5.6_spmd.clone, body=%wide.region_2.5_spmd.clone.sunk | while | flops 560607232 | bytes 76881064 | solution.py:133
  48.1 0.7 constant_dynamic-slice_fusion.4
  48.8 0.8 broadcast_compare_fusion.3
  49.6 3.2 %constant_dynamic-slice_fusion.5 = bf16[1,512,2048]{2,1,0:T(8,128)(2,1)} fusion(bf16[2,512,2048]{2,1,0:T(8,128)(2,1)} %get-tuple-element.210, s32[]{:T(128)} %get-tuple-element.194), kind=kLoop, calls=%fused_computation.13.clone.1 | loop fusion | bytes 4194308 | tf_op jit(solution)/shard_map/while/body/jit(dynamic_index_in_dim)/dynamic_slice | solution.py:133
  52.8 3.9 %copy.46 = bf16[1,512,2048]{1,2,0:T(8,128)(2,1)} copy(bf16[1,512,2048]{2,1,0:T(8,128)(2,1)} %constant_dynamic-slice_fusion.5) | data formatting | bytes 4194304 | tf_op jit(solution)/shard_map/while/body/jit(dynamic_index_in_dim)/dynamic_slice | solution.py:133
  56.7 2.6 %fusion.80 = (bf16[512,1024]{0,1:T(8,128)(2,1)}, bf16[512,1024]{0,1:T(8,128)(2,1)S(1)}) fusion(bf16[512,2048]{0,1:T(8,128)(2,1)} %bitcast.104), kind=kLoop, calls=%fused_computation.102.clone.1 | loop fusion | bytes 4194304 | tf_op jit(solution)/shard_map/while/body/eval_jaxpr/slice | solution.py:114
  59.3 1.5 fusion.81
  60.9 3.2 %copy-done.1 = f32[16,512,256]{2,1,0:T(8,128)} copy-done((f32[16,512,256]{2,1,0:T(8,128)}, f32[16,512,256]{2,1,0:T(8,128)S(1)}, u32[]{:S(2)}) %copy-start.1) | copy-done | bytes 8388632 | tf_op jit(solution)/shard_map/while
  64.0 2.3 %fusion.82 = f32[16,256]{1,0:T(8,128)} fusion(f32[16,512,256]{2,1,0:T(8,128)S(1)} %get-tuple-element.180, f32[16,256]{1,0:T(8,128)S(1)} %max.10, pred[256,512]{0,1:T(8,128)(4,1)S(1)} %broadcast_compare_fusion.3), kind=kLoop, calls=%fused_computation.4.clone.1 | loop fusion | flops 8384512 | bytes 8552448 | tf_op jit(solution)/shard_map/while/body/eval_jaxpr/reduce_sum | solution.py:124
  66.3 1.3 fusion.83
  67.7 7.0 %fusion.84 = f32[16,256,64]{1,2,0:T(8,128)} fusion(bf16[512,16,64]{0,2,1:T(8,128)(2,1)} %bitcast.106, f32[16,512,256]{2,1,0:T(8,128)} %copy-done.1, f32[16,256]{1,0:T(8,128)S(1)} %max.10, pred[256,512]{0,1:T(8,128)(4,1)S(1)} %broadcast_compare_fusion.3, f32[16,256,64]{1,2,0:T(8,128)} %get-tuple-element.197, f32[16,256]{1,0:T(8,128)S(1)} %get-tuple-element.183), kind=kOutput, calls=%fused_computation.8.clone.1 | convolution fusion | flops 277348352 | bytes 11698176 | tf_op jit(solution)/shard_map/while/body/eval_jaxpr/hrk,khd->hrd/dot_general | solution.py:125
  74.6 0.6 copy.64
  75.2 0.7 constant_dynamic-slice_fusion.4
  75.9 0.8 broadcast_compare_fusion.3
  76.7 3.2 %constant_dynamic-slice_fusion.5 = bf16[1,512,2048]{2,1,0:T(8,128)(2,1)} fusion(bf16[2,512,2048]{2,1,0:T(8,128)(2,1)} %get-tuple-element.210, s32[]{:T(128)} %get-tuple-element.194), kind=kLoop, calls=%fused_computation.13.clone.1 | loop fusion | bytes 4194308 | tf_op jit(solution)/shard_map/while/body/jit(dynamic_index_in_dim)/dynamic_slice | solution.py:133
  79.9 3.9 %copy.46 = bf16[1,512,2048]{1,2,0:T(8,128)(2,1)} copy(bf16[1,512,2048]{2,1,0:T(8,128)(2,1)} %constant_dynamic-slice_fusion.5) | data formatting | bytes 4194304 | tf_op jit(solution)/shard_map/while/body/jit(dynamic_index_in_dim)/dynamic_slice | solution.py:133
  83.8 2.6 %fusion.80 = (bf16[512,1024]{0,1:T(8,128)(2,1)}, bf16[512,1024]{0,1:T(8,128)(2,1)S(1)}) fusion(bf16[512,2048]{0,1:T(8,128)(2,1)} %bitcast.104), kind=kLoop, calls=%fused_computation.102.clone.1 | loop fusion | bytes 4194304 | tf_op jit(solution)/shard_map/while/body/eval_jaxpr/slice | solution.py:114
  86.5 1.5 fusion.81
  88.0 3.2 %copy-done.1 = f32[16,512,256]{2,1,0:T(8,128)} copy-done((f32[16,512,256]{2,1,0:T(8,128)}, f32[16,512,256]{2,1,0:T(8,128)S(1)}, u32[]{:S(2)}) %copy-start.1) | copy-done | bytes 8388632 | tf_op jit(solution)/shard_map/while
  91.2 2.3 %fusion.82 = f32[16,256]{1,0:T(8,128)} fusion(f32[16,512,256]{2,1,0:T(8,128)S(1)} %get-tuple-element.180, f32[16,256]{1,0:T(8,128)S(1)} %max.10, pred[256,512]{0,1:T(8,128)(4,1)S(1)} %broadcast_compare_fusion.3), kind=kLoop, calls=%fused_computation.4.clone.1 | loop fusion | flops 8384512 | bytes 8552448 | tf_op jit(solution)/shard_map/while/body/eval_jaxpr/reduce_sum | solution.py:124
  93.4 1.4 fusion.83
  94.8 7.0 %fusion.84 = f32[16,256,64]{1,2,0:T(8,128)} fusion(bf16[512,16,64]{0,2,1:T(8,128)(2,1)} %bitcast.106, f32[16,512,256]{2,1,0:T(8,128)} %copy-done.1, f32[16,256]{1,0:T(8,128)S(1)} %max.10, pred[256,512]{0,1:T(8,128)(4,1)S(1)} %broadcast_compare_fusion.3, f32[16,256,64]{1,2,0:T(8,128)} %get-tuple-element.197, f32[16,256]{1,0:T(8,128)S(1)} %get-tuple-element.183), kind=kOutput, calls=%fused_computation.8.clone.1 | convolution fusion | flops 277348352 | bytes 11698176 | tf_op jit(solution)/shard_map/while/body/eval_jaxpr/hrk,khd->hrd/dot_general | solution.py:125
  101.8 0.6 copy.64
  102.4 1.5 divide_convert_fusion
  103.9 2.7 %multiply_reduce_fusion.1 = (f32[256]{0:T(256)S(1)}, f32[256,1024]{1,0:T(8,128)S(1)}) fusion(bf16[256,1024]{0,1:T(8,128)(2,1)S(1)} %bitcast.111, bf16[1024,1024]{1,0:T(8,128)(2,1)} %param.22, bf16[256,1024]{1,0:T(8,128)(2,1)} %param.21), kind=kOutput, calls=%fused_computation.51 | convolution fusion | flops 537919232 | bytes 4195328 | tf_op jit(solution)/shard_map/dot_general | solution.py:141
  106.6 1.0 copy-done.2
  107.6 0.6 convolution_convert_fusion
  108.2 21.8 %all_to_all.10 = bf16[4,160,1024]{2,1,0:T(8,128)(2,1)S(1)} all-to-all(bf16[4,160,1024]{2,1,0:T(8,128)(2,1)S(1)} %bitcast.108), channel_id=1, replica_groups=mesh['expert'=4,'req'=8] {'expert'}, dimensions={0} | all-to-all | bytes 2621440 | tf_op jit(solution)/shard_map/all_to_all | solution.py:161
  130.0 3.9 %fusion.14 = f32[4,1,160,2816]{3,2,0,1:T(8,128)S(1)} fusion(bf16[4,160,1024]{2,1,0:T(8,128)(2,1)S(1)} %all_to_all.10, bf16[1,1024,2816]{2,1,0:T(8,128)(2,1)S(1)} %bitcast.119), kind=kOutput, calls=%fused_computation.20 | convolution fusion | flops 3690987520 | bytes 14286848 | tf_op jit(solution)/shard_map/slnd,ldf->slnf/dot_general | solution.py:166
  133.9 3.6 %fusion.34 = bf16[4,160,1024]{2,1,0:T(8,128)(2,1)} fusion(bf16[1,1408,1024]{2,1,0:T(8,128)(2,1)S(1)} %copy-done, f32[4,1,160,2816]{3,2,0,1:T(8,128)S(1)} %fusion.14), kind=kOutput, calls=%fused_computation.39 | convolution fusion | flops 1855160320 | bytes 11403264 | tf_op jit(solution)/shard_map/slnf,lfd->slnd/dot_general | solution.py:170
  137.6 4.3 %all-to-all-start.1 = ((bf16[4,160,1024]{2,1,0:T(8,128)(2,1)}), bf16[4,160,1024]{2,1,0:T(8,128)(2,1)}, u32[]{:S(2)}, u32[]{:S(2)}) async-start(bf16[4,160,1024]{2,1,0:T(8,128)(2,1)} %fusion.34), calls=%async_computation.1 | async-start | bytes 2621440 | tf_op jit(solution)/shard_map/all_to_all | solution.py:174
  141.9 1.5 fusion.56
  143.6 15.5 %all-to-all-done.1 = bf16[4,160,1024]{2,1,0:T(8,128)(2,1)} async-done(((bf16[4,160,1024]{2,1,0:T(8,128)(2,1)}), bf16[4,160,1024]{2,1,0:T(8,128)(2,1)}, u32[]{:S(2)}, u32[]{:S(2)}) %all-to-all-start.1) | async-done | bytes 1310752 | tf_op jit(solution)/shard_map/all_to_all | solution.py:174
  159.1 5.0 %gather_fusion = bf16[512,1024]{1,0:T(8,128)(2,1)} fusion(bf16[640,1024]{1,0:T(8,128)(2,1)} %bitcast.26, s32[1024]{0:T(1024)S(1)} %pad_clamp_fusion), kind=kCustom, calls=%fused_computation | custom fusion | bytes 2099200 | tf_op jit(solution)/shard_map/gather | solution.py:176
  164.1 1.6 fusion.28
  165.7 1.4 multiply_reduce_fusion
  167.1 1.0 multiply_convert_fusion
  (63 shorter events, 0.8 us)
Async XLA Ops:
  0.0 133.9 %copy-start = (bf16[1,1408,1024]{2,1,0:T(8,128)(2,1)S(1)}, bf16[1,1408,1024]{2,1,0:T(8,128)(2,1)}, u32[]{:S(2)}) copy-start(bf16[1,1408,1024]{2,1,0:T(8,128)(2,1)} %param.26) | copy-start | bytes 8650756
  0.0 6.4 %copy-start.15 = (s32[1,8]{1,0:T(1,128)S(1)}, s32[1,8]{1,0:T(1,128)}, u32[]{:S(2)}) copy-start(s32[1,8]{1,0:T(1,128)} %param.18) | copy-start | bytes 100
  0.0 7.2 %copy-start.7 = (s32[256,2]{0,1:T(2,128)S(1)}, s32[256,2]{0,1:T(2,128)}, u32[]{:S(2)}) copy-start(s32[256,2]{0,1:T(2,128)} %param.20) | copy-start | bytes 6148
  0.0 12.4 %collective-permute-start = (bf16[128,2048]{1,0:T(8,128)(2,1)}, bf16[128,2048]{1,0:T(8,128)(2,1)}, u32[]{:S(2)}, u32[]{:S(2)}) collective-permute-start(bf16[128,2048]{1,0:T(8,128)(2,1)} %bitcast.112), channel_id=1, source_target_pairs={{0,1},{1,2},{2,3},{3,4},{4,5},{5,6},{6,7},{7,0},{8,9},{9,10},{10,1... | collective-permute-start | bytes 1572872 | tf_op jit(solution)/shard_map/ppermute | solution.py:23
  0.1 15.6 %collective-permute-start.1 = (bf16[128,2048]{1,0:T(8,128)(2,1)}, bf16[128,2048]{1,0:T(8,128)(2,1)}, u32[]{:S(2)}, u32[]{:S(2)}) collective-permute-start(bf16[128,2048]{1,0:T(8,128)(2,1)} %bitcast.113), channel_id=1, source_target_pairs={{0,7},{1,0},{2,1},{3,2},{4,3},{5,4},{6,5},{7,6},{8,15},{9,8},{10,9... | collective-permute-start | bytes 1572872 | tf_op jit(solution)/shard_map/ppermute | solution.py:26
  8.4 12.7 %copy-start.13 = (bf16[1024]{0:T(1024)(128)(2,1)S(1)}, bf16[1024]{0:T(1024)(128)(2,1)}, u32[]{:S(2)}) copy-start(bf16[1024]{0:T(1024)(128)(2,1)} %param.23) | copy-start | bytes 6148
  8.7 19.6 %copy-start.9 = (s32[2,256]{1,0:T(2,128)}, s32[2,256]{1,0:T(2,128)S(1)}, u32[]{:S(2)}) copy-start(s32[2,256]{1,0:T(2,128)S(1)} %reshape.127) | copy-start | bytes 6148
  9.9 5.0 %copy-start.5 = (bf16[1,128,2048]{2,1,0:T(8,128)(2,1)S(1)}, bf16[1,128,2048]{2,1,0:T(8,128)(2,1)}, u32[]{:S(2)}) copy-start(bf16[1,128,2048]{2,1,0:T(8,128)(2,1)} %param.17) | copy-start | bytes 1572868
  12.4 9.3 %collective-permute-start.2 = (bf16[128,2048]{1,0:T(8,128)(2,1)}, bf16[128,2048]{1,0:T(8,128)(2,1)}, u32[]{:S(2)}, u32[]{:S(2)}) collective-permute-start(bf16[128,2048]{1,0:T(8,128)(2,1)} %collective-permute-done), channel_id=1, source_target_pairs={{0,1},{1,2},{2,3},{3,4},{4,5},{5,6},{6,7},{7,0},{8,9},{9,10},{10,1... | collective-permute-start | bytes 1572872 | tf_op jit(solution)/shard_map/ppermute | solution.py:23
  15.7 14.5 %collective-permute-start.3 = (bf16[128,2048]{1,0:T(8,128)(2,1)}, bf16[128,2048]{1,0:T(8,128)(2,1)}, u32[]{:S(2)}, u32[]{:S(2)}) collective-permute-start(bf16[128,2048]{1,0:T(8,128)(2,1)} %collective-permute-done.1), channel_id=1, source_target_pairs={{0,7},{1,0},{2,1},{3,2},{4,3},{5,4},{6,5},{7,6},{8,15},{9,8},{10,9... | collective-permute-start | bytes 1572872 | tf_op jit(solution)/shard_map/ppermute | solution.py:26
  21.7 11.9 %collective-permute-start.4 = (bf16[128,2048]{1,0:T(8,128)(2,1)}, bf16[128,2048]{1,0:T(8,128)(2,1)S(1)}, u32[]{:S(2)}, u32[]{:S(2)}) collective-permute-start(bf16[128,2048]{1,0:T(8,128)(2,1)} %collective-permute-done.2), channel_id=1, source_target_pairs={{0,1},{1,2},{2,3},{3,4},{4,5},{5,6},{6,7},{7,0},{8,9},{9,10},{10,1... | collective-permute-start | bytes 1572872 | tf_op jit(solution)/shard_map/ppermute | solution.py:23
  30.2 10.3 %collective-permute-start.5 = (bf16[128,2048]{1,0:T(8,128)(2,1)}, bf16[128,2048]{1,0:T(8,128)(2,1)S(1)}, u32[]{:S(2)}, u32[]{:S(2)}) collective-permute-start(bf16[128,2048]{1,0:T(8,128)(2,1)} %collective-permute-done.3), channel_id=1, source_target_pairs={{0,7},{1,0},{2,1},{3,2},{4,3},{5,4},{6,5},{7,6},{8,15},{9,8},{10,9... | collective-permute-start | bytes 1572872 | tf_op jit(solution)/shard_map/ppermute | solution.py:26
  33.6 13.7 %collective-permute-start.6 = (bf16[128,2048]{1,0:T(8,128)(2,1)S(1)}, bf16[128,2048]{1,0:T(8,128)(2,1)S(1)}, u32[]{:S(2)}, u32[]{:S(2)}) collective-permute-start(bf16[128,2048]{1,0:T(8,128)(2,1)S(1)} %collective-permute-done.4), channel_id=1, source_target_pairs={{0,1},{1,2},{2,3},{3,4},{4,5},{5,6},{6,7},{7,0},{8,9},{9,10},{10,1... | collective-permute-start | bytes 1572872 | tf_op jit(solution)/shard_map/ppermute | solution.py:23
  59.3 1.5 copy-start.3
  60.8 3.2 %copy-start.1 = (f32[16,512,256]{2,1,0:T(8,128)}, f32[16,512,256]{2,1,0:T(8,128)S(1)}, u32[]{:S(2)}) copy-start(f32[16,512,256]{2,1,0:T(8,128)S(1)} %get-tuple-element.180) | copy-start | bytes 25165828 | tf_op jit(solution)/shard_map/while
  86.5 1.5 copy-start.3
  87.9 3.2 %copy-start.1 = (f32[16,512,256]{2,1,0:T(8,128)}, f32[16,512,256]{2,1,0:T(8,128)S(1)}, u32[]{:S(2)}) copy-start(f32[16,512,256]{2,1,0:T(8,128)S(1)} %get-tuple-element.180) | copy-start | bytes 25165828 | tf_op jit(solution)/shard_map/while
  102.4 5.2 %copy-start.4 = (bf16[640,256]{1,0:T(8,128)(2,1)S(1)}, bf16[640,256]{1,0:T(8,128)(2,1)}, u32[]{:S(2)}) copy-start(bf16[640,256]{1,0:T(8,128)(2,1)} %fusion.43) | copy-start | bytes 983044
  102.4 5.2 %copy-start.6 = (f32[1024]{0:T(1024)S(1)}, f32[1024]{0:T(1024)}, u32[]{:S(2)}) copy-start(f32[1024]{0:T(1024)} %convert_element_type.81) | copy-start | bytes 12292
  102.4 27.6 %slice-start = ((s8[5767168]{0:T(1024)(128)(4,1)}), s8[4194304]{0:T(1024)(128)(4,1)S(1)}, s32[]{:S(2)}) async-start(s8[5767168]{0:T(1024)(128)(4,1)} %bitcast.118), calls=%async_computation.2 | async-start | bytes 8388608
  103.9 26.1 %slice-start.1 = ((s8[5767168]{0:T(1024)(128)(4,1)}), s8[1572864]{0:T(1024)(128)(4,1)S(1)}, s32[]{:S(2)}) async-start(s8[5767168]{0:T(1024)(128)(4,1)} %bitcast.118), calls=%async_computation.3 | async-start | bytes 3145728
  106.6 1.0 copy-start.2
  133.9 8.0 %copy-start.12 = (s32[1,2,2,128]{3,2,1,0:T(2,128)S(1)}, s32[1,2,2,128]{3,2,1,0:T(2,128)}, u32[]{:S(2)}) copy-start(s32[1,2,2,128]{3,2,1,0:T(2,128)} %get-tuple-element.113) | copy-start | bytes 6148
  133.9 8.0 %copy-start.14 = (bf16[1024]{0:T(1024)(128)(2,1)S(1)}, bf16[1024]{0:T(1024)(128)(2,1)}, u32[]{:S(2)}) copy-start(bf16[1024]{0:T(1024)(128)(2,1)} %param.27) | copy-start | bytes 6148
  133.9 8.0 %copy-start.11 = (bf16[1024,4]{0,1:T(4,128)(2,1)S(1)}, bf16[1024,4]{0,1:T(4,128)(2,1)}, u32[]{:S(2)}) copy-start(bf16[1024,4]{0,1:T(4,128)(2,1)} %param.24) | copy-start | bytes 24580
  133.9 9.5 %copy-start.8 = (s32[256,2]{0,1:T(2,128)S(1)}, s32[256,2]{0,1:T(2,128)}, u32[]{:S(2)}) copy-start(s32[256,2]{0,1:T(2,128)} %param.20) | copy-start | bytes 6148
  133.9 9.7 %copy-start.10 = (s32[2,256]{1,0:T(2,128)S(1)}, s32[2,256]{1,0:T(2,128)}, u32[]{:S(2)}) copy-start(s32[2,256]{1,0:T(2,128)} %copy-done.9) | copy-start | bytes 6148
  137.6 21.5 %all-to-all-start.1 = ((bf16[4,160,1024]{2,1,0:T(8,128)(2,1)}), bf16[4,160,1024]{2,1,0:T(8,128)(2,1)}, u32[]{:S(2)}, u32[]{:S(2)}) async-start(bf16[4,160,1024]{2,1,0:T(8,128)(2,1)} %fusion.34), calls=%async_computation.1 | async-start | bytes 2621440 | tf_op jit(solution)/shard_map/all_to_all | solution.py:174
